TPU v7x, 256 devices: a whole 4x4x8 slice. The times are simulated.
256 devices in a mesh: sib: 8 (over x_hi, y), wide: 32 (over x_lo, z, core).
Axes of the slice: x: 4 (x_hi: 2, x_lo: 2; x = x_hi * 2 + x_lo), y: 4, z: 8, core: 2. Of those that a mesh axis runs over, the one named last changes fastest.
Arguments:
- right_side: float32 [128, 32, 4096], P(None, 'wide', 'sib'), may hold values from -6 to 6
- tree_order: int32 [32, 4096], P('wide', 'sib'), may hold values from 0 to 4095, each once within a row
- x_start: float32 [128, 32, 4096], P(None, 'wide', 'sib'), may hold values from -6 to 6
- tangent_start: float32 [128, 32, 4096], P(None, 'wide', 'sib'), may hold values from -3 to 3
- dense_kernel: float32 [32, 8, 512, 512], P('wide', 'sib'), may hold values from -0.25 to 0.25
- dense_deriv: float32 [32, 8, 512, 512], P('wide', 'sib'), may hold values from -0.25 to 0.25
- leaf_basis: float32 [32, 8, 512, 256], P('wide', 'sib'), may hold values from -0.25 to 0.25
- transfer: float32 [32, 8, 256, 256], P('wide', 'sib'), may hold values from -0.375 to 0.375
- sibling_kernel: float32 [32, 8, 7, 256, 256], P('wide', 'sib'), may hold values from -0.125 to 0.125
- sibling_deriv: float32 [32, 8, 7, 256, 256], P('wide', 'sib'), may hold values from -0.125 to 0.125
- partner_list: int32 [32, 4], P('wide'), may hold values from 0 to 31, as said below
- parent_kernel: float32 [32, 4, 256, 256], P('wide'), may hold values from -0.1875 to 0.1875
- parent_deriv: float32 [32, 4, 256, 256], P('wide'), may hold values from -0.1875 to 0.1875
Outputs:
- solution: float32 [128, 32, 4096], P(None, 'wide', 'sib')
- tangent: float32 [128, 32, 4096], P(None, 'wide', 'sib')
Inputs may be any that keep to these rules, and one draw needn't show every extreme that they name: `partner_list`: row p names 4 different parent clusters, none of them p. `tree_order`: each row holds every position 0 .. 4095 once.
All inputs are finite; a program needn't handle non-finite values.
Results may differ from a plain program's by a relative error of at most 0.0001.
Values sent between devices are 32-bit elements; how exact they have to be, the bound alone decides.
A program may use at most 64 MiB of HBM per device.

v0:
```python
import jax
import jax.numpy as jnp
from jax import lax
from jax.sharding import PartitionSpec as P

ITERS = 2


highest = lax.Precision.HIGHEST
relax_step = 0.3
noise_level = 1.0


def copy_for_each(x, axis):
    copies = jnp.broadcast_to(x, (lax.axis_size(axis), *x.shape))
    return lax.all_to_all(copies, axis, split_axis=0, concat_axis=0, tiled=True)


def in_order(parts, dim):
    lengths = list(parts.shape[1:])
    lengths[dim] *= parts.shape[0]
    return jnp.moveaxis(parts, 0, dim).reshape(lengths)


def gather_directly(x, axis, dim):
    parts = copy_for_each(x, axis)
    return in_order(parts, dim)


def sent_together(arrays, axis, dim, along):
    both = jnp.concatenate(arrays, axis=along)
    out, at, finished = (lax.all_gather(both, axis, axis=dim, tiled=True), 0, [])
    for a in arrays:
        finished.append(lax.slice_in_dim(out, at, at + a.shape[along], axis=along))
        at += a.shape[along]
    return tuple(finished)


def split_up(x, dim, peers):
    lengths = x.shape
    parts = x.reshape(*lengths[:dim], peers, lengths[dim] // peers, *lengths[dim + 1 :])
    return jnp.moveaxis(parts, dim, 0)


def sum_at_owner(x, axis, dim):
    peers = lax.axis_size(axis)
    parts = lax.all_to_all(split_up(x, dim, peers), axis, 0, 0, tiled=True)
    return jnp.sum(parts, axis=0)


def sent_together_2(arrays, axis, dim, along):
    widths = [a.shape[along] for a in arrays]
    both = jnp.concatenate(arrays, axis=along)
    out = sum_at_owner(both, axis, dim)
    return tuple(jnp.split(out, [sum(widths[:k]) for k in range(1, len(widths))], axis=along))


def product(left, right):
    return jnp.dot(left, right, precision=highest, preferred_element_type=jnp.float32)


def product_t(left, right):
    return lax.dot_general(
        left, right, (((1,), (1,)), ((), ())), precision=highest, preferred_element_type=jnp.float32
    )


def body(
    right_side,
    tree_order,
    x_start,
    tangent_start,
    dense_kernel,
    dense_deriv,
    leaf_basis,
    transfer,
    sibling_kernel,
    sibling_deriv,
    partner_list,
    parent_kernel,
    parent_deriv,
):
    order = tree_order[0]
    dense = dense_kernel[0, 0]
    dense_d = dense_deriv[0, 0]
    basis = leaf_basis[0, 0]
    trans = transfer[0, 0]
    sib_k = sibling_kernel[0, 0]
    sib_d = sibling_deriv[0, 0]
    partners = partner_list[0]
    par_k = parent_kernel[0]
    par_d = parent_deriv[0]
    me = lax.axis_index("sib")
    count = lax.axis_size("sib")
    piece = gather_directly(right_side, "sib", 2)
    rows = piece.shape[2]
    inside = (order >= 0) & (order < rows)
    taken = jnp.take(piece[:, 0, :], jnp.clip(order, 0, rows - 1), axis=1)
    rhs = jnp.where(inside[None, :], taken, 0.0)
    x = x_start[:, 0, :]
    dx = tangent_start[:, 0, :]
    for step in range(ITERS):
        coeff_x = product(x, basis)
        coeff_dx = product(dx, basis)
        empty = jnp.zeros(coeff_x.shape, jnp.float32)
        term_x = product(coeff_x, trans)
        term_dx = product(coeff_dx, trans)
        start = jnp.int32(0)
        add_field_x = empty
        add_field_dx = empty
        add_piece_x, add_piece_dx = sent_together((coeff_x[None], coeff_dx[None]), "sib", 0, 1)
        for item in range(add_piece_x.shape[0]):
            other = start + item
            slot = jnp.clip((other - me - 1 + count) % count, 0, count - 2)
            weight = jnp.where(other == me, 0.0, 1.0).astype(jnp.float32)
            kern = lax.dynamic_index_in_dim(sib_k, slot, 0, keepdims=False)
            deriv = lax.dynamic_index_in_dim(sib_d, slot, 0, keepdims=False)
            add_field_x = add_field_x + weight * product(add_piece_x[item], kern)
            add_field_dx = add_field_dx + weight * (
                product(add_piece_x[item], deriv) + product(add_piece_dx[item], kern)
            )
        upper_x, upper_dx = sent_together_2((term_x, term_dx), "sib", 0, 1)
        piece_x, piece_dx = sent_together((upper_x[None], upper_dx[None]), "wide", 0, 1)
        index = jnp.arange(piece_x.shape[0], dtype=jnp.int32)
        select = (index[None, :] == partners[:, None]).astype(jnp.float32)
        chosen_x = jnp.einsum(
            "bn,nrk->brk", select, piece_x, precision=highest, preferred_element_type=jnp.float32
        )
        chosen_dx = jnp.einsum(
            "bn,nrk->brk", select, piece_dx, precision=highest, preferred_element_type=jnp.float32
        )
        field_x = jnp.einsum(
            "brk,bkm->rm", chosen_x, par_k, precision=highest, preferred_element_type=jnp.float32
        )
        field_dx = jnp.einsum(
            "brk,bkm->rm", chosen_x, par_d, precision=highest, preferred_element_type=jnp.float32
        ) + jnp.einsum(
            "brk,bkm->rm", chosen_dx, par_k, precision=highest, preferred_element_type=jnp.float32
        )
        far_x, far_dx = sent_together((field_x, field_dx), "sib", 0, 1)
        down_x = add_field_x + product_t(far_x, trans)
        down_dx = add_field_dx + product_t(far_dx, trans)
        image = product(x, dense) + product_t(down_x, basis)
        dimage = product(x, dense_d) + product(dx, dense) + product_t(down_dx, basis)
        x_next = x + relax_step * (rhs - noise_level * x - image)
        dx = dx - relax_step * (noise_level * dx + dimage)
        x = x_next
    return (x[:, None, :], dx[:, None, :])


def solution(mesh):
    placed = (
        P(None, "wide", "sib"),
        P("wide", "sib"),
        P(None, "wide", "sib"),
        P(None, "wide", "sib"),
        P("wide", "sib", None, None),
        P("wide", "sib", None, None),
        P("wide", "sib", None, None),
        P("wide", "sib", None, None),
        P("wide", "sib", None, None, None),
        P("wide", "sib", None, None, None),
        P("wide", None),
        P("wide", None, None, None),
        P("wide", None, None, None),
    )
    return jax.shard_map(
        body,
        mesh=mesh,
        in_specs=placed,
        out_specs=(P(None, "wide", "sib"), P(None, "wide", "sib")),
        check_vma=False,
    )
```

profile of v0, /device:TPU:1, one launch (start us, length us, event | category | flops | bytes accessed | tf_op | source)
XLA Modules:
  0.0 334.7 jit_solution(11184319112064550893)
XLA Ops:
  7.2 1.7 fusion.92
  8.9 1.6 fusion.94
  10.5 1.2 fusion.141
  12.1 14.9 %all_to_all.15 = f32[8,16,512]{2,1,0:T(8,128)S(1)} all-to-all(f32[8,16,512]{2,1,0:T(8,128)S(1)} %bitcast.375), channel_id=1, replica_groups=mesh['sib'=8,'wide'=32] {'sib'}, dimensions={0} | all-to-all | bytes 524288 | tf_op jit(solution)/shard_map/all_to_all | solution.py:47
  27.0 0.6 pad_maximum_fusion.4
  27.6 0.7 pad_maximum_fusion
  28.5 1.5 broadcast_in_dim.63
  30.1 4.5 %all-to-all-start = ((f32[8,128,1,512]{1,3,2,0:T(8,128)}), f32[8,128,1,512]{1,3,2,0:T(8,128)}, u32[]{:S(2)}, u32[]{:S(2)}) async-start(f32[8,128,1,512]{1,3,2,0:T(8,128)} %broadcast_in_dim.63), calls=%async_computation | async-start | bytes 4194304 | tf_op jit(solution)/shard_map/all_to_all | solution.py:16
  34.9 1.9 fusion.62
  36.8 1.4 fusion.74
  38.2 1.4 convolution_add_fusion.5
  39.6 21.1 %all-to-all-done = f32[8,128,1,512]{1,3,2,0:T(8,128)} async-done(((f32[8,128,1,512]{1,3,2,0:T(8,128)}), f32[8,128,1,512]{1,3,2,0:T(8,128)}, u32[]{:S(2)}, u32[]{:S(2)}) %all-to-all-start) | async-done | bytes 2097184 | tf_op jit(solution)/shard_map/all_to_all | solution.py:16
  60.8 3.3 gather_fusion
  64.1 1.9 copy.36
  65.9 26.1 %all-gather.7.cloned.1.call-done = f32[32,32,256]{2,1,0:T(8,128)} async-done(((f32[1,32,256]{2,1,0:T(8,128)}), f32[32,32,256]{2,1,0:T(8,128)}) %all-gather.7.cloned.1.call-update) | async-done | bytes 1048592 | tf_op jit(solution)/shard_map/all_gather | solution.py:32
  92.0 1.4 fusion.294
  93.4 0.6 fusion.82
  94.0 0.5 convolution_bitcast_fusion.4
  94.5 0.5 convolution_bitcast_fusion.5
  95.0 0.6 fusion.80
  95.6 0.5 fusion.59
  96.2 28.7 %all_gather.20 = f32[128,512]{1,0:T(8,128)S(1)} all-gather(f32[16,512]{1,0:T(8,128)S(1)} %pad_maximum_fusion.5), channel_id=1, replica_groups=mesh['sib'=8,'wide'=32] {'sib'}, dimensions={0}, use_global_device_ids=true | all-gather | bytes 294912 | tf_op jit(solution)/shard_map/all_gather | solution.py:32
  124.9 28.5 %all-gather.5.cloned.1.call-done = f32[8,256,256]{2,1,0:T(8,128)} async-done(((f32[1,256,256]{2,1,0:T(8,128)}), f32[8,256,256]{2,1,0:T(8,128)}) %all-gather.5.cloned.1.call-update) | async-done | bytes 2097168 | tf_op jit(solution)/shard_map/all_gather | solution.py:32
  153.4 1.4 fusion.131
  154.8 1.3 fusion.127
  156.1 1.3 fusion.123
  157.4 1.3 fusion.119
  158.8 1.2 fusion.115
  160.0 1.2 fusion.111
  161.2 1.2 fusion.107
  162.4 1.2 fusion.103
  166.1 0.4 convolution_add_fusion.16
  166.5 0.6 fusion.11
  167.2 0.4 fusion.86
  170.5 0.7 fusion.13
  171.2 0.4 fusion.89
  172.2 10.7 %all_to_all.16 = f32[8,16,512]{2,1,0:T(8,128)} all-to-all(f32[8,16,512]{2,1,0:T(8,128)S(1)} %bitcast.376), channel_id=1, replica_groups=mesh['sib'=8,'wide'=32] {'sib'}, dimensions={0} | all-to-all | bytes 524288 | tf_op jit(solution)/shard_map/all_to_all | solution.py:47
  182.8 1.0 reduce_sum.19
  183.8 0.6 pad_maximum_fusion.6
  184.7 0.7 pad_maximum_fusion.2
  185.5 2.0 fusion.60
  187.5 1.4 fusion.72
  189.0 1.4 convolution_add_fusion.4
  190.4 57.3 %all-gather.11.cloned.1.call-done = f32[32,32,256]{2,1,0:T(8,128)} async-done(((f32[1,32,256]{2,1,0:T(8,128)}), f32[32,32,256]{2,1,0:T(8,128)}) %all-gather.11.cloned.1.call-update) | async-done | bytes 1048592 | tf_op jit(solution)/shard_map/all_gather | solution.py:32
  247.7 1.4 fusion.293
  249.1 0.6 fusion.78
  249.7 0.5 convolution_bitcast_fusion.1
  250.3 0.5 convolution_bitcast_fusion.2
  250.8 0.6 fusion.76
  251.4 0.5 fusion.58
  251.9 28.5 %all_gather.23 = f32[128,512]{1,0:T(8,128)S(1)} all-gather(f32[16,512]{1,0:T(8,128)S(1)} %pad_maximum_fusion.7), channel_id=1, replica_groups=mesh['sib'=8,'wide'=32] {'sib'}, dimensions={0}, use_global_device_ids=true | all-gather | bytes 294912 | tf_op jit(solution)/shard_map/all_gather | solution.py:32
  280.5 28.5 %all-gather.9.cloned.1.call-done = f32[8,256,256]{2,1,0:T(8,128)} async-done(((f32[1,256,256]{2,1,0:T(8,128)}), f32[8,256,256]{2,1,0:T(8,128)}) %all-gather.9.cloned.1.call-update) | async-done | bytes 2097168 | tf_op jit(solution)/shard_map/all_gather | solution.py:32
  309.0 1.4 fusion.129
  310.4 1.3 fusion.125
  311.7 1.3 fusion.121
  313.0 1.3 fusion.117
  314.4 1.2 fusion.113
  315.6 1.2 fusion.109
  316.8 1.2 fusion.105
  318.0 1.2 fusion.101
  322.0 0.6 fusion.6
  322.7 1.0 copy.48
  326.6 0.7 fusion.9
  327.2 1.0 copy.47
  (113 shorter events, 12.4 us)
Async XLA Ops:
  7.2 156.4 %copy-start = (f32[1,1,7,256,256]{4,3,2,1,0:T(8,128)S(1)}, f32[1,1,7,256,256]{4,3,2,1,0:T(8,128)}, u32[]{:S(2)}) copy-start(f32[1,1,7,256,256]{4,3,2,1,0:T(8,128)} %param.21) | copy-start | bytes 5505028
  7.2 4.6 %copy-start.2 = (f32[1,1,256,256]{3,2,1,0:T(8,128)S(1)}, f32[1,1,256,256]{3,2,1,0:T(8,128)}, u32[]{:S(2)}) copy-start(f32[1,1,256,256]{3,2,1,0:T(8,128)} %param.20) | copy-start | bytes 786436
  7.2 84.8 %all-gather.7.cloned.1.call-start = ((), (), s32[]{:S(2)}) async-start(), calls=%async_computation.4 | async-start | bytes 1081344 | tf_op jit(solution)/shard_map/all_gather | solution.py:32
  8.9 19.5 %copy-start.24 = (f32[128,1,512]{2,1,0:T(1,128)S(1)}, f32[128,1,512]{2,1,0:T(1,128)}, u32[]{:S(2)}) copy-start(f32[128,1,512]{2,1,0:T(1,128)} %param.13) | copy-start | bytes 786436
  27.6 125.8 %all-gather.5.cloned.1.call-start = ((), (), s32[]{:S(2)}) async-start(), calls=%async_computation.3 | async-start | bytes 2359296 | tf_op jit(solution)/shard_map/all_gather | solution.py:32
  30.1 4.7 %copy-start.25 = (s32[1,512]{1,0:T(1,128)S(1)}, s32[1,512]{1,0:T(1,128)}, u32[]{:S(2)}) copy-start(s32[1,512]{1,0:T(1,128)} %param.14) | copy-start | bytes 6148
  30.1 4.8 %copy-start.13 = (f32[128,1,512]{2,1,0:T(1,128)S(1)}, f32[128,1,512]{2,1,0:T(1,128)}, u32[]{:S(2)}) copy-start(f32[128,1,512]{2,1,0:T(1,128)} %param.15) | copy-start | bytes 786436
  30.1 6.7 %copy-start.3 = (f32[1,1,512,512]{3,2,1,0:T(8,128)S(1)}, f32[1,1,512,512]{3,2,1,0:T(8,128)}, u32[]{:S(2)}) copy-start(f32[1,1,512,512]{3,2,1,0:T(8,128)} %param.17) | copy-start | bytes 3145732
  30.1 30.7 %all-to-all-start = ((f32[8,128,1,512]{1,3,2,0:T(8,128)}), f32[8,128,1,512]{1,3,2,0:T(8,128)}, u32[]{:S(2)}, u32[]{:S(2)}) async-start(f32[8,128,1,512]{1,3,2,0:T(8,128)} %broadcast_in_dim.63), calls=%async_computation | async-start | bytes 4194304 | tf_op jit(solution)/shard_map/all_to_all | solution.py:16
  34.6 213.1 %all-gather.11.cloned.1.call-start = ((), (), s32[]{:S(2)}) async-start(), calls=%async_computation.6 | async-start | bytes 1081344 | tf_op jit(solution)/shard_map/all_gather | solution.py:32
  34.8 3.5 %copy-start.14 = (f32[128,1,512]{2,1,0:T(1,128)S(1)}, f32[128,1,512]{2,1,0:T(1,128)}, u32[]{:S(2)}) copy-start(f32[128,1,512]{2,1,0:T(1,128)} %param.16) | copy-start | bytes 786436
  60.8 32.6 %copy-start.26 = (s32[1,4]{1,0:T(1,128)S(1)}, s32[1,4]{1,0:T(1,128)}, u32[]{:S(2)}) copy-start(s32[1,4]{1,0:T(1,128)} %param.23) | copy-start | bytes 52
  64.1 30.5 %copy-start.5 = (f32[1,4,256,256]{3,2,1,0:T(8,128)S(1)}, f32[1,4,256,256]{3,2,1,0:T(8,128)}, u32[]{:S(2)}) copy-start(f32[1,4,256,256]{3,2,1,0:T(8,128)} %param.24) | copy-start | bytes 3145732
  92.0 2.0 copy-start.11
  124.9 41.2 %copy-start.18 = (f32[128,512]{1,0:T(8,128)}, f32[128,512]{1,0:T(8,128)S(1)}, u32[]{:S(2)}) copy-start(f32[128,512]{1,0:T(8,128)S(1)} %all_gather.20) | copy-start | bytes 786436
  153.4 5.4 %copy-start.7 = (f32[1,1,7,256,256]{4,3,2,1,0:T(8,128)S(1)}, f32[1,1,7,256,256]{4,3,2,1,0:T(8,128)}, u32[]{:S(2)}) copy-start(f32[1,1,7,256,256]{4,3,2,1,0:T(8,128)} %param.22) | copy-start | bytes 5505028
  153.4 10.2 %copy-start.9 = (f32[8,256,256]{2,1,0:T(8,128)S(1)}, f32[8,256,256]{2,1,0:T(8,128)}, u32[]{:S(2)}) copy-start(f32[8,256,256]{2,1,0:T(8,128)} %all-gather.5.cloned.1.call-done) | copy-start | bytes 6291460
  164.8 1.7 copy-start.1
  164.8 1.7 copy-start.15
  164.8 1.7 copy-start.20
  168.2 1.9 copy-start.19
  168.5 2.0 copy-start.16
  168.5 2.0 copy-start.23
  184.5 124.5 %all-gather.9.cloned.1.call-start = ((), (), s32[]{:S(2)}) async-start(), calls=%async_computation.5 | async-start | bytes 2359296 | tf_op jit(solution)/shard_map/all_gather | solution.py:32
  185.5 2.0 copy-start.4
  247.7 2.0 copy-start.12
  247.7 2.6 copy-start.6
  309.0 5.4 %copy-start.8 = (f32[1,1,7,256,256]{4,3,2,1,0:T(8,128)S(1)}, f32[1,1,7,256,256]{4,3,2,1,0:T(8,128)}, u32[]{:S(2)}) copy-start(f32[1,1,7,256,256]{4,3,2,1,0:T(8,128)} %param.22) | copy-start | bytes 5505028
  309.0 10.2 %copy-start.10 = (f32[8,256,256]{2,1,0:T(8,128)S(1)}, f32[8,256,256]{2,1,0:T(8,128)}, u32[]{:S(2)}) copy-start(f32[8,256,256]{2,1,0:T(8,128)} %all-gather.9.cloned.1.call-done) | copy-start | bytes 6291460
  320.4 1.6 copy-start.21
  324.6 2.0 copy-start.17
  324.6 2.0 copy-start.22
Sparse Core Ops, SparseCore 0:
  27.7 64.2 all-gather.6
  95.2 58.0 all-gather.4
  184.6 63.0 all-gather.10
  250.8 58.1 all-gather.8
where the time goes:
time: 335 us
  waiting for transfers between devices  162 us (48%)
  blocking collectives  82.7 us (25%)
  matrix products  55.2 us (16%)
  between operations  14.9 us (4%)
  local copies, waits for them, and re-layouts  11.7 us (3%)
  starting transfers between devices  4.86 us (1%)
  other arithmetic  3.76 us (1%)
    all_gather x4, waiting for transfers between devices, sent_together(): lax.all_gather(both, axis, axis=dim, tiled=True)  140 us
    all_gather x2, blocking collectives, sent_together(): lax.all_gather(both, axis, axis=dim, tiled=True)  57.2 us
    dot_general x62, matrix products, product(): jnp.dot(left, right, precision=highest, preferred_element_type=jnp.float32)  45.5 us
    all_to_all x2, blocking collectives, sum_at_owner(): parts = lax.all_to_all(split_up(x, dim, peers), axis, 0, 0, tiled=True)  25.5 us
    all_to_all x1, waiting for transfers between devices, copy_for_each(): return lax.all_to_all(copies, axis, split_axis=0, concat_axis=0, tiled=True)  21.1 us
  transfers between devices with their start and end apart: 5, of which 5 were waited for; matrix products, arithmetic and copies ran while one was open for 8% of the time, Pallas kernels for 0%

commit v1 on v0

v1 whole, which is shorter than its diff:
```python
import functools

import jax
import jax.numpy as jnp
from jax import lax
from jax.experimental import pallas as pl
from jax.experimental.pallas import tpu as pltpu
from jax.sharding import PartitionSpec as P

ITERS = 2
N_SIB = 8
N_Z = 8
LEAF = 512
RHS = 128
RANK = 256
NB_PAR = 4
PARENTS = 32
ROWS = RHS // N_SIB
LANES = 128

relax_step = 0.3
noise_level = 1.0

f32 = jnp.float32
bf16 = jnp.bfloat16
MESH = pl.DeviceIdType.MESH

SIB_ORDER = (1, 7, 4, 3, 5, 2, 6)
Z_ORDER = (0, 1, 7, 2, 6, 3, 5, 4)


def parts(v):
    high = v.astype(bf16)
    return high, (v - high.astype(f32)).astype(bf16)


def dot(left, right):
    return jnp.dot(left, right, preferred_element_type=f32)


def dot_t(left, right):
    return lax.dot_general(left, right, (((1,), (1,)), ((), ())), preferred_element_type=f32)


def product(left, right, op=dot):
    lh, ll = left
    rh, rl = right
    rows = lh.shape[0]
    both = op(jnp.concatenate([lh, ll], axis=0), rh)
    return both[:rows] + (both[rows:] + op(lh, rl))


def kernel(
    rhs_hbm, order_hbm, x_hbm, dx_hbm, dense_hbm, dense_d_hbm, basis_hbm, trans_hbm, sib_k_hbm, sib_d_hbm,
    partners, par_k_hbm, par_d_hbm,
    x_out, dx_out,
    x_in, dx_in, dense_in, dense_d_in, basis_in, trans_in, sib_k_in, sib_d_in, par_k_in, par_d_in,
    dense_h, dense_l, dense_d_h, dense_d_l, basis_h, basis_l, trans_h, trans_l,
    sib_k_h, sib_k_l, sib_d_h, sib_d_l, par_k_h, par_k_l, par_d_h, par_d_l,
    state, coeff, coeff_in, term, term_in, upper_0, upper_1, field,
    points_in, points, order, placed, rhs,
    load_sem, coeff_s, coeff_r, term_s, term_r, field_s, field_r,
    z_s, z_r, xlo_s, xlo_r, core_s, core_r, rhs_s, rhs_r, order_s, order_r, back_s, back_r,
):
    me = lax.axis_index("sib")
    wide = lax.axis_index("wide")
    xlo, z, core = wide // 16, wide // 2 % N_Z, wide % 2

    def sib_at(o):
        return lax.rem(me + o, N_SIB)

    def sib_dev(o):
        return (sib_at(o), wide)

    def parent(xl, zz, cc):
        return xl * 16 + lax.rem(zz + N_Z, N_Z) * 2 + cc

    loads = {}

    def load(name, src, dst, k):
        loads[name] = pltpu.make_async_copy(src, dst, load_sem.at[k])
        loads[name].start()

    load("x", x_hbm, x_in, 0)
    load("basis", basis_hbm.at[0, 0], basis_in, 1)
    load("dx", dx_hbm, dx_in, 2)
    load("trans", trans_hbm.at[0, 0], trans_in, 3)
    load("points", rhs_hbm.at[pl.ds(pl.multiple_of(me * ROWS, ROWS), ROWS)], points_in.at[me], 4)
    load("order", order_hbm, order.at[me], 5)
    load("dense", dense_hbm.at[0, 0], dense_in, 6)
    load("dense_d", dense_d_hbm.at[0, 0], dense_d_in, 7)
    load("par_k", par_k_hbm.at[0], par_k_in, 8)
    load("par_d", par_d_hbm.at[0], par_d_in, 9)
    load("sib_k", sib_k_hbm.at[0, 0], sib_k_in, 10)
    load("sib_d", sib_d_hbm.at[0, 0], sib_d_in, 11)

    barrier = pltpu.get_barrier_semaphore()

    def greet(device):
        pl.semaphore_signal(barrier, inc=1, device_id=device, device_id_type=MESH)

    for o in range(1, N_SIB):
        greet(sib_dev(o))
    for d in range(1, N_Z):
        greet((me, parent(xlo, z + d, core)))
    greet((me, parent(1 - xlo, z, core)))
    greet((me, parent(xlo, z, 1 - core)))

    sent = []

    def send(src, dst, ssem, rsem, device):
        c = pltpu.make_async_remote_copy(
            src_ref=src, dst_ref=dst, send_sem=ssem, recv_sem=rsem, device_id=device, device_id_type=MESH
        )
        c.start()
        sent.append(c)
        return c

    def split(src, high, low):
        h, l = parts(src)
        high[...] = h
        low[...] = l

    def coefficients(it):
        v = parts(state[it])
        c = product(v, (basis_h[...], basis_l[...]))
        coeff[it] = c
        t = product(parts(c), (trans_h[...], trans_l[...]))
        for s in range(N_SIB):
            term[it, s, :ROWS] = t[s * ROWS:(s + 1) * ROWS]
            term[it, s, ROWS:] = t[RHS + s * ROWS:RHS + (s + 1) * ROWS]

    loads["x"].wait()
    state[0, :RHS] = x_in[...].reshape(RHS, LEAF)
    loads["basis"].wait()
    split(basis_in[...], basis_h, basis_l)
    loads["dx"].wait()
    state[0, RHS:] = dx_in[...].reshape(RHS, LEAF)
    loads["trans"].wait()
    split(trans_in[...], trans_h, trans_l)
    coefficients(0)

    pl.semaphore_wait(barrier, 7 + 7 + 2)

    for it in range(ITERS):
        last = it == ITERS - 1
        upper = (upper_0, upper_1)[it]
        for o in SIB_ORDER:
            send(term.at[it, sib_at(o)], term_in.at[it, o - 1], term_s.at[it, o - 1], term_r.at[it, o - 1], sib_dev(o))
        if it == 0:
            loads["points"].wait()
            loads["order"].wait()
            for o in SIB_ORDER:
                send(order.at[me], order.at[me], order_s.at[o - 1], order_r.at[o - 1], sib_dev(o))
                send(
                    rhs_hbm.at[pl.ds(pl.multiple_of(sib_at(o) * ROWS, ROWS), ROWS)], points_in.at[me],
                    rhs_s.at[o - 1], rhs_r.at[o - 1], sib_dev(o),
                )
        for o in SIB_ORDER:
            send(
                coeff.at[it], coeff_in.at[it, o - 1], coeff_s.at[it, o - 1], coeff_r.at[it, o - 1],
                sib_dev(N_SIB - o),
            )

        def arrived(buf, sem):
            pltpu.make_async_copy(buf, buf, sem).wait()

        if it == 0:
            loads["dense"].wait()
            split(dense_in[...], dense_h, dense_l)
            loads["dense_d"].wait()
            split(dense_d_in[...], dense_d_h, dense_d_l)
        vh, vl = parts(state[it])
        own = product((vh, vl), (dense_h[...], dense_l[...]))
        own_d = product((vh[:RHS], vl[:RHS]), (dense_d_h[...], dense_d_l[...]))
        state[it + 1, :RHS] = own[:RHS]
        state[it + 1, RHS:] = own[RHS:] + own_d

        total = term[it, me]
        for o in SIB_ORDER:
            arrived(term_in.at[it, o - 1], term_r.at[it, o - 1])
            total = total + term_in[it, o - 1]
        upper[wide] = total

        def to_xlo(d):
            at = parent(xlo, z - d, core)
            send(upper.at[at], upper.at[at], xlo_s.at[it, d], xlo_r.at[it, d], (me, parent(1 - xlo, z, core)))

        def to_core(xl, far, d):
            at = parent(xl, z - d, core)
            send(
                upper.at[at], upper.at[at], core_s.at[it, far * N_Z + d], core_r.at[it, far * N_Z + d],
                (me, parent(xlo, z, 1 - core)),
            )

        for d in Z_ORDER[1:]:
            send(
                upper.at[wide], upper.at[wide], z_s.at[it, d - 1], z_r.at[it, d - 1],
                (me, parent(xlo, z + d, core)),
            )
        to_xlo(0)
        to_core(xlo, 0, 0)

        if it == 0:
            loads["par_k"].wait()
            split(par_k_in[...], par_k_h, par_k_l)
            loads["par_d"].wait()
            split(par_d_in[...], par_d_h, par_d_l)
            loads["sib_k"].wait()
            loads["sib_d"].wait()

            for o in SIB_ORDER:
                arrived(order.at[sib_at(o)], order_r.at[N_SIB - o - 1])
                arrived(points_in.at[sib_at(o)], rhs_r.at[N_SIB - o - 1])
            for s in range(N_SIB):
                seg = points_in[s].reshape(ROWS, LEAF)
                for q in range(LEAF // LANES):
                    points[s * (LEAF // LANES) + q] = seg[:, q * LANES:(q + 1) * LANES]

            def place(s, _):
                want_all = order[s]
                for q in range(LEAF // LANES):
                    want = jnp.broadcast_to(want_all[:, q * LANES:(q + 1) * LANES], (ROWS, LANES))
                    block = want // LANES
                    lane = want % LANES
                    got = jnp.zeros((ROWS, LANES), f32)
                    for b in range(PARENTS):
                        found = jnp.take_along_axis(points[b], lane, axis=1, mode="promise_in_bounds")
                        got = jnp.where(block == b, found, got)
                    placed[s, :, q * LANES:(q + 1) * LANES] = got
                return 0

            lax.fori_loop(0, N_SIB, place, 0)
            rhs[me] = placed[me]
            for o in SIB_ORDER:
                send(placed.at[sib_at(o)], rhs.at[me], back_s.at[o - 1], back_r.at[o - 1], sib_dev(o))

        def from_z(d):
            if d:
                at = upper.at[parent(xlo, z - d, core)]
                arrived(at, z_r.at[it, d - 1])
                to_xlo(d)
                to_core(xlo, 0, d)

        def from_xlo(d):
            arrived(upper.at[parent(1 - xlo, z - d, core)], xlo_r.at[it, d])
            to_core(1 - xlo, 1, d)

        for k in range(N_Z + 2):
            if k < N_Z:
                from_z(Z_ORDER[k])
            if k >= 2:
                from_xlo(Z_ORDER[k - 2])
        for far in range(2):
            for d in Z_ORDER:
                arrived(
                    upper.at[parent(far + xlo - 2 * far * xlo, z - d, 1 - core)], core_r.at[it, far * N_Z + d]
                )

        hx = jnp.zeros((ROWS, RANK), f32)
        hd = jnp.zeros((ROWS, RANK), f32)
        for k in range(NB_PAR):
            ch, cl = parts(upper[partners[0, k]])
            kk = product((ch, cl), (par_k_h[k], par_k_l[k]))
            kd = product((ch[:ROWS], cl[:ROWS]), (par_d_h[k], par_d_l[k]))
            hx = hx + kk[:ROWS]
            hd = hd + (kk[ROWS:] + kd)
        field[it, me, :ROWS] = hx
        field[it, me, ROWS:] = hd
        for o in SIB_ORDER:
            send(field.at[it, me], field.at[it, me], field_s.at[it, o - 1], field_r.at[it, o - 1], sib_dev(o))

        gx = jnp.zeros((2 * RHS, RANK), f32)
        gd = jnp.zeros((RHS, RANK), f32)
        for o in SIB_ORDER:
            if it == 0:
                split(sib_k_in[o - 1], sib_k_h.at[o - 1], sib_k_l.at[o - 1])
                split(sib_d_in[o - 1], sib_d_h.at[o - 1], sib_d_l.at[o - 1])
            arrived(coeff_in.at[it, o - 1], coeff_r.at[it, o - 1])
            ah, al = parts(coeff_in[it, o - 1])
            gx = gx + product((ah, al), (sib_k_h[o - 1], sib_k_l[o - 1]))
            gd = gd + product((ah[:RHS], al[:RHS]), (sib_d_h[o - 1], sib_d_l[o - 1]))

        for o in SIB_ORDER:
            arrived(field.at[it, sib_at(o)], field_r.at[it, N_SIB - o - 1])
        h = jnp.concatenate(
            [field[it, :, :ROWS].reshape(RHS, RANK), field[it, :, ROWS:].reshape(RHS, RANK)], axis=0
        )
        down = product(parts(h), (trans_h[...], trans_l[...]), dot_t) + gx
        down = jnp.concatenate([down[:RHS], down[RHS:] + gd], axis=0)
        image = state[it + 1] + product(parts(down), (basis_h[...], basis_l[...]), dot_t)
        if it == 0:
            for o in SIB_ORDER:
                arrived(rhs.at[sib_at(o)], back_r.at[N_SIB - o - 1])
        x = state[it, :RHS]
        dx = state[it, RHS:]
        x_next = x + relax_step * (rhs[...].reshape(RHS, LEAF) - noise_level * x - image[:RHS])
        dx_next = dx - relax_step * (noise_level * dx + image[RHS:])
        if last:
            x_out[...] = x_next.reshape(RHS, 1, LEAF)
            dx_out[...] = dx_next.reshape(RHS, 1, LEAF)
        else:
            state[it + 1, :RHS] = x_next
            state[it + 1, RHS:] = dx_next
            coefficients(it + 1)

    for c in sent:
        c.wait_send()


def body(*args):
    V = pltpu.VMEM
    D = pltpu.SemaphoreType.DMA
    any_space = pl.BlockSpec(memory_space=pl.ANY)
    specs = [any_space] * 13
    specs[10] = pl.BlockSpec(memory_space=pltpu.SMEM)
    out = jax.ShapeDtypeStruct((RHS, 1, LEAF), f32)
    weights = [(LEAF, LEAF)] * 2 + [(LEAF, RANK), (RANK, RANK)] + [(N_SIB - 1, RANK, RANK)] * 2 + [(NB_PAR, RANK, RANK)] * 2
    scratch = [V((RHS, 1, LEAF), f32)] * 2
    scratch += [V(w, f32) for w in weights]
    for w in weights:
        scratch += [V(w, bf16)] * 2
    scratch += [
        V((ITERS + 1, 2 * RHS, LEAF), f32),
        V((ITERS, 2 * RHS, RANK), f32),
        V((ITERS, N_SIB - 1, 2 * RHS, RANK), f32),
        V((ITERS, N_SIB, 2 * ROWS, RANK), f32),
        V((ITERS, N_SIB - 1, 2 * ROWS, RANK), f32),
        V((PARENTS, 2 * ROWS, RANK), f32),
        V((PARENTS, 2 * ROWS, RANK), f32),
        V((ITERS, N_SIB, 2 * ROWS, RANK), f32),
        V((N_SIB, ROWS, 1, LEAF), f32),
        V((PARENTS, ROWS, LANES), f32),
        V((N_SIB, 1, LEAF), jnp.int32),
        V((N_SIB, ROWS, LEAF), f32),
        V((N_SIB, ROWS, LEAF), f32),
        D((12,)),
    ]
    peers = N_SIB - 1
    scratch += [D((ITERS, peers))] * 6
    scratch += [D((ITERS, N_Z - 1))] * 2 + [D((ITERS, N_Z))] * 2 + [D((ITERS, 2 * N_Z))] * 2
    scratch += [D((peers,))] * 6
    return pl.pallas_call(
        kernel,
        out_shape=(out, out),
        in_specs=specs,
        out_specs=(pl.BlockSpec(memory_space=pltpu.VMEM), pl.BlockSpec(memory_space=pltpu.VMEM)),
        scratch_shapes=scratch,
        compiler_params=pltpu.CompilerParams(
            collective_id=0, has_side_effects=True, vmem_limit_bytes=52 * 1024 * 1024
        ),
        name="richardson",
    )(*args)


def solution(mesh):
    placed = (
        P(None, "wide", "sib"),
        P("wide", "sib"),
        P(None, "wide", "sib"),
        P(None, "wide", "sib"),
        P("wide", "sib", None, None),
        P("wide", "sib", None, None),
        P("wide", "sib", None, None),
        P("wide", "sib", None, None),
        P("wide", "sib", None, None, None),
        P("wide", "sib", None, None, None),
        P("wide", None),
        P("wide", None, None, None),
        P("wide", None, None, None),
    )
    return jax.shard_map(
        body,
        mesh=mesh,
        in_specs=placed,
        out_specs=(P(None, "wide", "sib"), P(None, "wide", "sib")),
        check_vma=False,
    )
```

time: 335 us -> 117 us (0.35)
  waiting for transfers between devices: 162 us -> 0 us
  Pallas kernels: 0 us -> 109 us
  blocking collectives: 82.7 us -> 0 us
  matrix products: 55.2 us -> 0 us
  between operations: 14.9 us -> 0.66 us
  local copies, waits for them, and re-layouts: 11.7 us -> 6.53 us
  starting transfers between devices: 4.86 us -> 0 us
  other arithmetic: 3.76 us -> 0 us
    all_gather x4 -> x0, waiting for transfers between devices: 140 us -> none  [sent_together(): lax.all_gather(both, axis, axis=dim, tiled=True)]
    pallas_call x0 -> x1, Pallas kernels: none -> 109 us  [body(): pl.pallas_call(kernel, out_shape=(out, out), in_specs=specs, out_specs=(p...]
    all_gather x2 -> x0, blocking collectives: 57.2 us -> none  [sent_together(): lax.all_gather(both, axis, axis=dim, tiled=True)]
    dot_general x80 -> x0, matrix products: 55.2 us -> none  [the longest x62 45.5 us: product(): jnp.dot(left, right, precision=highest, preferred_element_type=jnp.float32)]
    all_to_all x2 -> x0, blocking collectives: 25.5 us -> none  [sum_at_owner(): parts = lax.all_to_all(split_up(x, dim, peers), axis, 0, 0, tiled=True)]
    all_to_all x1 -> x0, waiting for transfers between devices: 21.1 us -> none  [copy_for_each(): return lax.all_to_all(copies, axis, split_axis=0, concat_axis=0, tiled=True)]
    gather x2 -> x0, local copies, waits for them, and re-layouts: 5.14 us -> none  [body(): taken = jnp.take(piece[:, 0, :], jnp.clip(order, 0, rows - 1), axis=1)]
    all_to_all x1 -> x0, starting transfers between devices: 4.47 us -> none  [copy_for_each(): return lax.all_to_all(copies, axis, split_axis=0, concat_axis=0, tiled=True)]
  transfers between devices with their start and end apart: 5 -> 0, of which waited for: 5 -> 0; matrix products, arithmetic and copies ran while one was open for 8% -> 0% of each run, Pallas kernels for 0% -> 0%
where the time goes in v1:
time: 117 us; the launch traced here: 116 us
  Pallas kernels  109 us (93%)
  local copies, waits for them, and re-layouts  6.53 us (6%)
    pallas_call x1, Pallas kernels, body(): pl.pallas_call(kernel, out_shape=(out, out), in_specs=specs, out_specs=(p...  109 us
    unnamed x14, local copies, waits for them, and re-layouts  6.53 us

profile of v1, /device:TPU:1, one launch (start us, length us, event | category | flops | bytes accessed | tf_op | source)
XLA Modules:
  0.0 116.4 jit_solution(7100917110637447440)
XLA Ops:
  0.6 0.0 copy-start
  0.6 0.9 copy-done
  1.6 0.0 copy-start.1
  1.6 0.9 copy-done.1
  2.5 0.0 copy-start.2
  2.5 0.9 copy-done.2
  3.5 0.0 copy-start.3
  3.5 0.9 copy-done.3
  4.4 0.0 copy-start.4
  4.4 0.7 copy-done.4
  5.1 0.0 copy-start.5
  5.1 0.7 copy-done.5
  5.8 109.2 %richardson.1 = (f32[128,1,512]{2,1,0:T(1,128)S(1)}, f32[128,1,512]{2,1,0:T(1,128)S(1)}) custom-call(f32[128,1,512]{2,1,0:T(1,128)S(1)} %copy-done, s32[1,512]{1,0:T(1,128)S(1)} %copy-done.4, f32[128,1,512]{2,1,0:T(1,128)S(1)} %copy-done.1, f32[128,1,512]{2,1,0:T(1,128)S(1)} %copy-done.2, f32[1,1,512,512]{3,2,1,0:T(8,128)} %dense_hbm.1, ...), custom_call_target="tpu_custom_call" | custom-call | tf_op jit(solution)/shard_map/richardson/pallas_call | solution.py:343
  115.0 0.7 copy.17
  115.7 0.7 copy.18
Async XLA Ops:
  0.6 1.0 copy-start
  1.6 0.9 copy-start.1
  2.5 0.9 copy-start.2
  3.5 0.9 copy-start.3
  4.4 0.7 copy-start.4
  5.1 0.7 copy-start.5

commit v2 on v1

--- a/solution.py
+++ b/solution.py
@@ -26,6 +26,7 @@
 MESH = pl.DeviceIdType.MESH
 
 SIB_ORDER = (1, 7, 4, 3, 5, 2, 6)
+BLOCKS = ((1, 0), (0, -1), (0, 1), (1, -1), (1, 1), (0, 2), (1, 2))
 Z_ORDER = (0, 1, 7, 2, 6, 3, 5, 4)
 
 
@@ -52,13 +53,13 @@
 
 def kernel(
     rhs_hbm, order_hbm, x_hbm, dx_hbm, dense_hbm, dense_d_hbm, basis_hbm, trans_hbm, sib_k_hbm, sib_d_hbm,
-    partners, par_k_hbm, par_d_hbm,
+    partners_hbm, par_k_hbm, par_d_hbm,
     x_out, dx_out,
     x_in, dx_in, dense_in, dense_d_in, basis_in, trans_in, sib_k_in, sib_d_in, par_k_in, par_d_in,
     dense_h, dense_l, dense_d_h, dense_d_l, basis_h, basis_l, trans_h, trans_l,
     sib_k_h, sib_k_l, sib_d_h, sib_d_l, par_k_h, par_k_l, par_d_h, par_d_l,
     state, coeff, coeff_in, term, term_in, upper_0, upper_1, field,
-    points_in, points, order, placed, rhs,
+    points_in, points, order, placed, rhs, partners,
     load_sem, coeff_s, coeff_r, term_s, term_r, field_s, field_r,
     z_s, z_r, xlo_s, xlo_r, core_s, core_r, rhs_s, rhs_r, order_s, order_r, back_s, back_r,
 ):
@@ -71,6 +72,13 @@
 
     def sib_dev(o):
         return (sib_at(o), wide)
+
+    xhi, y = me // 4, me % 4
+
+    def near(dx, dy):
+        return lax.rem(xhi + dx, 2) * 4 + lax.rem(y + dy + 4, 4)
+
+    across, y_next, y_prev = (near(1, 0), wide), (near(0, 1), wide), (near(0, -1), wide)
 
     def parent(xl, zz, cc):
         return xl * 16 + lax.rem(zz + N_Z, N_Z) * 2 + cc
@@ -89,6 +97,7 @@
     load("order", order_hbm, order.at[me], 5)
     load("dense", dense_hbm.at[0, 0], dense_in, 6)
     load("dense_d", dense_d_hbm.at[0, 0], dense_d_in, 7)
+    load("partners", partners_hbm, partners, 12)
     load("par_k", par_k_hbm.at[0], par_k_in, 8)
     load("par_d", par_d_hbm.at[0], par_d_in, 9)
     load("sib_k", sib_k_hbm.at[0, 0], sib_k_in, 10)
@@ -115,6 +124,12 @@
         c.start()
         sent.append(c)
         return c
+
+    def arrived(buf, sem):
+        pltpu.make_async_copy(buf, buf, sem).wait()
+
+    def slot(dx, dy):
+        return dx % 2 * 4 + dy % 4
 
     def split(src, high, low):
         h, l = parts(src)
@@ -156,14 +171,23 @@
                     rhs_hbm.at[pl.ds(pl.multiple_of(sib_at(o) * ROWS, ROWS), ROWS)], points_in.at[me],
                     rhs_s.at[o - 1], rhs_r.at[o - 1], sib_dev(o),
                 )
-        for o in SIB_ORDER:
-            send(
-                coeff.at[it], coeff_in.at[it, o - 1], coeff_s.at[it, o - 1], coeff_r.at[it, o - 1],
-                sib_dev(N_SIB - o),
-            )
-
-        def arrived(buf, sem):
-            pltpu.make_async_copy(buf, buf, sem).wait()
+        gathered = []
+
+        def piece(dx, dy, half):
+            return coeff_in.at[it, slot(dx, dy), pl.ds(half * RHS, RHS)]
+
+        def pass_on(src, dx, dy, half, device):
+            send(src, piece(dx, dy, half), coeff_s.at[it, len(gathered)], coeff_r.at[it, slot(dx, dy), half], device)
+            gathered.append(None)
+
+        def have(dx, dy, half):
+            arrived(piece(dx, dy, half), coeff_r.at[it, slot(dx, dy), half])
+
+        for half in range(2):
+            mine = coeff.at[it, pl.ds(half * RHS, RHS)]
+            pass_on(mine, 1, 0, half, across)
+            pass_on(mine, 0, -1, half, y_next)
+            pass_on(mine, 0, 1, half, y_prev)
 
         if it == 0:
             loads["dense"].wait()
@@ -201,6 +225,11 @@
         to_xlo(0)
         to_core(xlo, 0, 0)
 
+        for half in range(2):
+            have(1, 0, half)
+            pass_on(piece(1, 0, half), 1, -1, half, y_next)
+            pass_on(piece(1, 0, half), 1, 1, half, y_prev)
+
         if it == 0:
             loads["par_k"].wait()
             split(par_k_in[...], par_k_h, par_k_l)
@@ -208,6 +237,9 @@
             split(par_d_in[...], par_d_h, par_d_l)
             loads["sib_k"].wait()
             loads["sib_d"].wait()
+            for k in range(N_SIB - 1):
+                split(sib_k_in[k], sib_k_h.at[k], sib_k_l.at[k])
+                split(sib_d_in[k], sib_d_h.at[k], sib_d_l.at[k])
 
             for o in SIB_ORDER:
                 arrived(order.at[sib_at(o)], order_r.at[N_SIB - o - 1])
@@ -246,17 +278,28 @@
             arrived(upper.at[parent(1 - xlo, z - d, core)], xlo_r.at[it, d])
             to_core(1 - xlo, 1, d)
 
+        def opposite(dx):
+            have(dx, -1, 0)
+            pass_on(piece(dx, -1, 0), dx, 2, 0, y_next)
+            have(dx, 1, 1)
+            pass_on(piece(dx, 1, 1), dx, 2, 1, y_prev)
+
         for k in range(N_Z + 2):
             if k < N_Z:
                 from_z(Z_ORDER[k])
+            if k == 3:
+                opposite(0)
             if k >= 2:
                 from_xlo(Z_ORDER[k - 2])
+        opposite(1)
         for far in range(2):
             for d in Z_ORDER:
                 arrived(
                     upper.at[parent(far + xlo - 2 * far * xlo, z - d, 1 - core)], core_r.at[it, far * N_Z + d]
                 )
 
+        if it == 0:
+            loads["partners"].wait()
         hx = jnp.zeros((ROWS, RANK), f32)
         hd = jnp.zeros((ROWS, RANK), f32)
         for k in range(NB_PAR):
@@ -272,14 +315,14 @@
 
         gx = jnp.zeros((2 * RHS, RANK), f32)
         gd = jnp.zeros((RHS, RANK), f32)
-        for o in SIB_ORDER:
-            if it == 0:
-                split(sib_k_in[o - 1], sib_k_h.at[o - 1], sib_k_l.at[o - 1])
-                split(sib_d_in[o - 1], sib_d_h.at[o - 1], sib_d_l.at[o - 1])
-            arrived(coeff_in.at[it, o - 1], coeff_r.at[it, o - 1])
-            ah, al = parts(coeff_in[it, o - 1])
-            gx = gx + product((ah, al), (sib_k_h[o - 1], sib_k_l[o - 1]))
-            gd = gd + product((ah[:RHS], al[:RHS]), (sib_d_h[o - 1], sib_d_l[o - 1]))
+        for dx, dy in BLOCKS:
+            for half in range(2):
+                if dy == 2 or dy == 1 and half == 0 or dy == -1 and half == 1:
+                    have(dx, dy, half)
+            at = lax.rem(near(dx, dy) - me + N_SIB, N_SIB) - 1
+            ah, al = parts(coeff_in[it, slot(dx, dy)])
+            gx = gx + product((ah, al), (sib_k_h[at], sib_k_l[at]))
+            gd = gd + product((ah[:RHS], al[:RHS]), (sib_d_h[at], sib_d_l[at]))
 
         for o in SIB_ORDER:
             arrived(field.at[it, sib_at(o)], field_r.at[it, N_SIB - o - 1])
@@ -311,9 +354,7 @@
 def body(*args):
     V = pltpu.VMEM
     D = pltpu.SemaphoreType.DMA
-    any_space = pl.BlockSpec(memory_space=pl.ANY)
-    specs = [any_space] * 13
-    specs[10] = pl.BlockSpec(memory_space=pltpu.SMEM)
+    specs = [pl.BlockSpec(memory_space=pltpu.HBM)] * 13
     out = jax.ShapeDtypeStruct((RHS, 1, LEAF), f32)
     weights = [(LEAF, LEAF)] * 2 + [(LEAF, RANK), (RANK, RANK)] + [(N_SIB - 1, RANK, RANK)] * 2 + [(NB_PAR, RANK, RANK)] * 2
     scratch = [V((RHS, 1, LEAF), f32)] * 2
@@ -323,7 +364,7 @@
     scratch += [
         V((ITERS + 1, 2 * RHS, LEAF), f32),
         V((ITERS, 2 * RHS, RANK), f32),
-        V((ITERS, N_SIB - 1, 2 * RHS, RANK), f32),
+        V((ITERS, N_SIB, 2 * RHS, RANK), f32),
         V((ITERS, N_SIB, 2 * ROWS, RANK), f32),
         V((ITERS, N_SIB - 1, 2 * ROWS, RANK), f32),
         V((PARENTS, 2 * ROWS, RANK), f32),
@@ -334,10 +375,11 @@
         V((N_SIB, 1, LEAF), jnp.int32),
         V((N_SIB, ROWS, LEAF), f32),
         V((N_SIB, ROWS, LEAF), f32),
-        D((12,)),
+        pltpu.SMEM((1, NB_PAR), jnp.int32),
+        D((13,)),
     ]
     peers = N_SIB - 1
-    scratch += [D((ITERS, peers))] * 6
+    scratch += [D((ITERS, 14)), D((ITERS, N_SIB, 2))] + [D((ITERS, peers))] * 4
     scratch += [D((ITERS, N_Z - 1))] * 2 + [D((ITERS, N_Z))] * 2 + [D((ITERS, 2 * N_Z))] * 2
     scratch += [D((peers,))] * 6
     return pl.pallas_call(
@@ -347,7 +389,7 @@
         out_specs=(pl.BlockSpec(memory_space=pltpu.VMEM), pl.BlockSpec(memory_space=pltpu.VMEM)),
         scratch_shapes=scratch,
         compiler_params=pltpu.CompilerParams(
-            collective_id=0, has_side_effects=True, vmem_limit_bytes=52 * 1024 * 1024
+            collective_id=0, has_side_effects=True, vmem_limit_bytes=63 * 1024 * 1024
         ),
         name="richardson",
     )(*args)

time: 117 us -> 86.6 us (0.74)
  Pallas kernels: 109 us -> 82.5 us
  local copies, waits for them, and re-layouts: 6.53 us -> 3.34 us
    pallas_call x1, Pallas kernels: 109 us -> 82.5 us  [body(): pl.pallas_call(kernel, out_shape=(out, out), in_specs=specs, out_specs=(p...]
    unnamed x14 -> x2, local copies, waits for them, and re-layouts: 6.53 us -> 3.34 us
where the time goes in v2:
time: 86.6 us; the launch traced here: 86.5 us
  Pallas kernels  82.5 us (95%)
  local copies, waits for them, and re-layouts  3.34 us (4%)
    pallas_call x1, Pallas kernels, body(): pl.pallas_call(kernel, out_shape=(out, out), in_specs=specs, out_specs=(p...  82.5 us
    unnamed x2, local copies, waits for them, and re-layouts  3.34 us

profile of v2, /device:TPU:1, one launch (start us, length us, event | category | flops | bytes accessed | tf_op | source)
XLA Modules:
  0.0 86.5 jit_solution(15705112804595729148)
XLA Ops:
  0.6 82.5 %richardson.1 = (f32[128,1,512]{2,1,0:T(1,128)}, f32[128,1,512]{2,1,0:T(1,128)}) custom-call(f32[128,1,512]{2,1,0:T(1,128)} %rhs_hbm.1, s32[1,512]{1,0:T(1,128)} %order_hbm.1, f32[128,1,512]{2,1,0:T(1,128)} %x_hbm.1, f32[128,1,512]{2,1,0:T(1,128)} %dx_hbm.1, f32[1,1,512,512]{3,2,1,0:T(8,128)} %dense_hbm.1, f32[1,1,512,512]{3,2,1,0:T(8,128)} %dense_d_hbm.1, ...), custom_call_target="tpu_custom_call" | custom-call | tf_op jit(solution)/shard_map/richardson/pallas_call | solution.py:385
  83.1 1.7 %copy.17 = f32[128,1,512]{2,1,0:T(1,128)} copy(f32[128,1,512]{2,1,0:T(1,128)} %get-tuple-element.4) | data formatting | bytes 524288
  84.8 1.7 %copy.18 = f32[128,1,512]{2,1,0:T(1,128)} copy(f32[128,1,512]{2,1,0:T(1,128)} %get-tuple-element.5) | data formatting | bytes 524288

commit v3 on v2

--- a/solution.py
+++ b/solution.py
@@ -27,7 +27,9 @@
 
 SIB_ORDER = (1, 7, 4, 3, 5, 2, 6)
 BLOCKS = ((1, 0), (0, -1), (0, 1), (1, -1), (1, 1), (0, 2), (1, 2))
-Z_ORDER = (0, 1, 7, 2, 6, 3, 5, 4)
+Z_ORDER = (1, 7, 2, 6, 3, 5, 4)
+TO_XLO = ((3, 3), (6, 1), (2, 1), (7, 1), (1, 1), (0, 1))
+TO_CORE = ((3, 3), (6, 2), (1, 2), (0, 1))
 
 
 def parts(v):
@@ -57,8 +59,9 @@
     x_out, dx_out,
     x_in, dx_in, dense_in, dense_d_in, basis_in, trans_in, sib_k_in, sib_d_in, par_k_in, par_d_in,
     dense_h, dense_l, dense_d_h, dense_d_l, basis_h, basis_l, trans_h, trans_l,
+    pair_h, pair_l, lift_h, lift_l, turn_h, turn_l,
     sib_k_h, sib_k_l, sib_d_h, sib_d_l, par_k_h, par_k_l, par_d_h, par_d_l,
-    state, coeff, coeff_in, term, term_in, upper_0, upper_1, field,
+    state, ahead, coeff, coeff_in, term, term_in, upper_0, upper_1, field,
     points_in, points, order, placed, rhs, partners,
     load_sem, coeff_s, coeff_r, term_s, term_r, field_s, field_r,
     z_s, z_r, xlo_s, xlo_r, core_s, core_r, rhs_s, rhs_r, order_s, order_r, back_s, back_r,
@@ -139,8 +142,10 @@
     def coefficients(it):
         v = parts(state[it])
         c = product(v, (basis_h[...], basis_l[...]))
+        keep(it, c, product(parts(c), (trans_h[...], trans_l[...])))
+
+    def keep(it, c, t):
         coeff[it] = c
-        t = product(parts(c), (trans_h[...], trans_l[...]))
         for s in range(N_SIB):
             term[it, s, :ROWS] = t[s * ROWS:(s + 1) * ROWS]
             term[it, s, ROWS:] = t[RHS + s * ROWS:RHS + (s + 1) * ROWS]
@@ -194,53 +199,60 @@
             split(dense_in[...], dense_h, dense_l)
             loads["dense_d"].wait()
             split(dense_d_in[...], dense_d_h, dense_d_l)
-        vh, vl = parts(state[it])
+            loads["par_k"].wait()
+            split(par_k_in[...], par_k_h, par_k_l)
+            loads["par_d"].wait()
+            split(par_d_in[...], par_d_h, par_d_l)
+        else:
+            state[it] = ahead[...] - relax_step * product(field_parts, (lift_h[...], lift_l[...]))
+        v = state[it]
+        vh, vl = parts(v)
         own = product((vh, vl), (dense_h[...], dense_l[...]))
         own_d = product((vh[:RHS], vl[:RHS]), (dense_d_h[...], dense_d_l[...]))
-        state[it + 1, :RHS] = own[:RHS]
-        state[it + 1, RHS:] = own[RHS:] + own_d
+        ahead[:RHS] = v[:RHS] - relax_step * (noise_level * v[:RHS] + own[:RHS])
+        ahead[RHS:] = v[RHS:] - relax_step * (noise_level * v[RHS:] + (own[RHS:] + own_d))
 
         total = term[it, me]
         for o in SIB_ORDER:
             arrived(term_in.at[it, o - 1], term_r.at[it, o - 1])
             total = total + term_in[it, o - 1]
-        upper[wide] = total
-
-        def to_xlo(d):
-            at = parent(xlo, z - d, core)
-            send(upper.at[at], upper.at[at], xlo_s.at[it, d], xlo_r.at[it, d], (me, parent(1 - xlo, z, core)))
-
-        def to_core(xl, far, d):
-            at = parent(xl, z - d, core)
+        upper[core, xlo, 4] = total
+
+        for d in Z_ORDER:
             send(
-                upper.at[at], upper.at[at], core_s.at[it, far * N_Z + d], core_r.at[it, far * N_Z + d],
-                (me, parent(xlo, z, 1 - core)),
-            )
-
-        for d in Z_ORDER[1:]:
-            send(
-                upper.at[wide], upper.at[wide], z_s.at[it, d - 1], z_r.at[it, d - 1],
+                upper.at[core, xlo, 4], upper.at[core, xlo, (d + 4) % N_Z], z_s.at[it, d - 1], z_r.at[it, d - 1],
                 (me, parent(xlo, z + d, core)),
             )
-        to_xlo(0)
-        to_core(xlo, 0, 0)
-
-        for half in range(2):
+
+        def to_xlo(k):
+            run = upper.at[core, xlo, pl.ds(*TO_XLO[k])]
+            send(run, run, xlo_s.at[it, k], xlo_r.at[it, k], (me, parent(1 - xlo, z, core)))
+
+        def to_core(far, k):
+            run = upper.at[core, far + xlo - 2 * far * xlo, pl.ds(*TO_CORE[k])]
+            send(run, run, core_s.at[it, far, k], core_r.at[it, far, k], (me, parent(xlo, z, 1 - core)))
+
+        def from_z(d):
+            arrived(upper.at[core, xlo, (d + 4) % N_Z], z_r.at[it, d - 1])
+
+        def from_xlo(k):
+            arrived(upper.at[core, 1 - xlo, pl.ds(*TO_XLO[k])], xlo_r.at[it, k])
+
+        def from_core(far, k):
+            arrived(upper.at[1 - core, far + xlo - 2 * far * xlo, pl.ds(*TO_CORE[k])], core_r.at[it, far, k])
+
+        def onward(half):
             have(1, 0, half)
             pass_on(piece(1, 0, half), 1, -1, half, y_next)
             pass_on(piece(1, 0, half), 1, 1, half, y_prev)
 
-        if it == 0:
-            loads["par_k"].wait()
-            split(par_k_in[...], par_k_h, par_k_l)
-            loads["par_d"].wait()
-            split(par_d_in[...], par_d_h, par_d_l)
-            loads["sib_k"].wait()
-            loads["sib_d"].wait()
-            for k in range(N_SIB - 1):
-                split(sib_k_in[k], sib_k_h.at[k], sib_k_l.at[k])
-                split(sib_d_in[k], sib_d_h.at[k], sib_d_l.at[k])
-
+        def opposite(dx):
+            have(dx, -1, 0)
+            pass_on(piece(dx, -1, 0), dx, 2, 0, y_next)
+            have(dx, 1, 1)
+            pass_on(piece(dx, 1, 1), dx, 2, 1, y_prev)
+
+        def points_here():
             for o in SIB_ORDER:
                 arrived(order.at[sib_at(o)], order_r.at[N_SIB - o - 1])
                 arrived(points_in.at[sib_at(o)], rhs_r.at[N_SIB - o - 1])
@@ -249,61 +261,87 @@
                 for q in range(LEAF // LANES):
                     points[s * (LEAF // LANES) + q] = seg[:, q * LANES:(q + 1) * LANES]
 
-            def place(s, _):
-                want_all = order[s]
-                for q in range(LEAF // LANES):
-                    want = jnp.broadcast_to(want_all[:, q * LANES:(q + 1) * LANES], (ROWS, LANES))
-                    block = want // LANES
-                    lane = want % LANES
-                    got = jnp.zeros((ROWS, LANES), f32)
-                    for b in range(PARENTS):
-                        found = jnp.take_along_axis(points[b], lane, axis=1, mode="promise_in_bounds")
-                        got = jnp.where(block == b, found, got)
-                    placed[s, :, q * LANES:(q + 1) * LANES] = got
-                return 0
-
-            lax.fori_loop(0, N_SIB, place, 0)
+        def place(s, _):
+            want_all = order[s]
+            for q in range(LEAF // LANES):
+                want = jnp.broadcast_to(want_all[:, q * LANES:(q + 1) * LANES], (ROWS, LANES))
+                block = want // LANES
+                lane = want % LANES
+                got = jnp.zeros((ROWS, LANES), f32)
+                for b in range(PARENTS):
+                    found = jnp.take_along_axis(points[b], lane, axis=1, mode="promise_in_bounds")
+                    got = jnp.where(block == b, found, got)
+                placed[s, :, q * LANES:(q + 1) * LANES] = got
+            return 0
+
+        def place_two(k):
+            if it == 0:
+                lax.fori_loop(2 * k, 2 * k + 2, place, 0)
+
+        def split_sib(first, end):
+            if it == 0:
+                for k in range(first, end):
+                    split(sib_k_in[k], sib_k_h.at[k], sib_k_l.at[k])
+                    split(sib_d_in[k], sib_d_h.at[k], sib_d_l.at[k])
+
+        onward(0)
+        onward(1)
+        if it == 0:
+            loads["sib_k"].wait()
+            loads["sib_d"].wait()
+        split_sib(0, 2)
+        from_z(1)
+        from_z(7)
+        to_xlo(0)
+        to_core(0, 0)
+        if it == 0:
+            points_here()
+        from_z(2)
+        to_xlo(1)
+        from_z(6)
+        to_xlo(2)
+        place_two(0)
+        from_xlo(0)
+        to_core(1, 0)
+        opposite(0)
+        from_z(3)
+        to_xlo(3)
+        to_core(0, 1)
+        place_two(1)
+        from_z(5)
+        to_xlo(4)
+        to_core(0, 2)
+        place_two(2)
+        from_z(4)
+        to_xlo(5)
+        to_core(0, 3)
+        opposite(1)
+        from_xlo(1)
+        from_xlo(3)
+        to_core(1, 1)
+        place_two(3)
+        if it == 0:
             rhs[me] = placed[me]
             for o in SIB_ORDER:
                 send(placed.at[sib_at(o)], rhs.at[me], back_s.at[o - 1], back_r.at[o - 1], sib_dev(o))
-
-        def from_z(d):
-            if d:
-                at = upper.at[parent(xlo, z - d, core)]
-                arrived(at, z_r.at[it, d - 1])
-                to_xlo(d)
-                to_core(xlo, 0, d)
-
-        def from_xlo(d):
-            arrived(upper.at[parent(1 - xlo, z - d, core)], xlo_r.at[it, d])
-            to_core(1 - xlo, 1, d)
-
-        def opposite(dx):
-            have(dx, -1, 0)
-            pass_on(piece(dx, -1, 0), dx, 2, 0, y_next)
-            have(dx, 1, 1)
-            pass_on(piece(dx, 1, 1), dx, 2, 1, y_prev)
-
-        for k in range(N_Z + 2):
-            if k < N_Z:
-                from_z(Z_ORDER[k])
-            if k == 3:
-                opposite(0)
-            if k >= 2:
-                from_xlo(Z_ORDER[k - 2])
-        opposite(1)
+        from_xlo(2)
+        from_xlo(4)
+        to_core(1, 2)
+        from_xlo(5)
+        to_core(1, 3)
+        split_sib(2, N_SIB - 1)
+        if it == 0:
+            loads["partners"].wait()
         for far in range(2):
-            for d in Z_ORDER:
-                arrived(
-                    upper.at[parent(far + xlo - 2 * far * xlo, z - d, 1 - core)], core_r.at[it, far * N_Z + d]
-                )
-
-        if it == 0:
-            loads["partners"].wait()
+            for k in range(len(TO_CORE)):
+                from_core(far, k)
+
         hx = jnp.zeros((ROWS, RANK), f32)
         hd = jnp.zeros((ROWS, RANK), f32)
         for k in range(NB_PAR):
-            ch, cl = parts(upper[partners[0, k]])
+            who = partners[0, k]
+            found = upper[who % 2, who // 16, lax.rem(z - who // 2 % N_Z + N_Z + 4, N_Z)]
+            ch, cl = parts(found)
             kk = product((ch, cl), (par_k_h[k], par_k_l[k]))
             kd = product((ch[:ROWS], cl[:ROWS]), (par_d_h[k], par_d_l[k]))
             hx = hx + kk[:ROWS]
@@ -312,6 +350,12 @@
         field[it, me, ROWS:] = hd
         for o in SIB_ORDER:
             send(field.at[it, me], field.at[it, me], field_s.at[it, o - 1], field_r.at[it, o - 1], sib_dev(o))
+
+        if it == 0:
+            both = product((basis_h[...], basis_l[...]), (trans_h[...], trans_l[...]))
+            split(jnp.concatenate([basis_in[...], both], axis=1), pair_h, pair_l)
+            split(both.T, lift_h, lift_l)
+            split(product((lift_h[...], lift_l[...]), (pair_h[...], pair_l[...])), turn_h, turn_l)
 
         gx = jnp.zeros((2 * RHS, RANK), f32)
         gd = jnp.zeros((RHS, RANK), f32)
@@ -323,32 +367,37 @@
             ah, al = parts(coeff_in[it, slot(dx, dy)])
             gx = gx + product((ah, al), (sib_k_h[at], sib_k_l[at]))
             gd = gd + product((ah[:RHS], al[:RHS]), (sib_d_h[at], sib_d_l[at]))
+        near_field = jnp.concatenate([gx[:RHS], gx[RHS:] + gd], axis=0)
+        known = ahead[...] - relax_step * product(parts(near_field), (basis_h[...], basis_l[...]), dot_t)
+        if it == 0:
+            for o in SIB_ORDER:
+                arrived(rhs.at[sib_at(o)], back_r.at[N_SIB - o - 1])
+        ahead[:RHS] = known[:RHS] + relax_step * rhs[...].reshape(RHS, LEAF)
+        ahead[RHS:] = known[RHS:]
+        if not last:
+            known_c = product(parts(ahead[...]), (pair_h[...], pair_l[...]))
 
         for o in SIB_ORDER:
             arrived(field.at[it, sib_at(o)], field_r.at[it, N_SIB - o - 1])
         h = jnp.concatenate(
             [field[it, :, :ROWS].reshape(RHS, RANK), field[it, :, ROWS:].reshape(RHS, RANK)], axis=0
         )
-        down = product(parts(h), (trans_h[...], trans_l[...]), dot_t) + gx
-        down = jnp.concatenate([down[:RHS], down[RHS:] + gd], axis=0)
-        image = state[it + 1] + product(parts(down), (basis_h[...], basis_l[...]), dot_t)
-        if it == 0:
-            for o in SIB_ORDER:
-                arrived(rhs.at[sib_at(o)], back_r.at[N_SIB - o - 1])
-        x = state[it, :RHS]
-        dx = state[it, RHS:]
-        x_next = x + relax_step * (rhs[...].reshape(RHS, LEAF) - noise_level * x - image[:RHS])
-        dx_next = dx - relax_step * (noise_level * dx + image[RHS:])
+        field_parts = parts(h)
         if last:
-            x_out[...] = x_next.reshape(RHS, 1, LEAF)
-            dx_out[...] = dx_next.reshape(RHS, 1, LEAF)
+            result = ahead[...] - relax_step * product(field_parts, (lift_h[...], lift_l[...]))
+            x_out[...] = result[:RHS].reshape(RHS, 1, LEAF)
+            dx_out[...] = result[RHS:].reshape(RHS, 1, LEAF)
         else:
-            state[it + 1, :RHS] = x_next
-            state[it + 1, RHS:] = dx_next
-            coefficients(it + 1)
+            next_c = known_c - relax_step * product(field_parts, (turn_h[...], turn_l[...]))
+            keep(it + 1, next_c[:, :RANK], next_c[:, RANK:])
 
     for c in sent:
         c.wait_send()
+
+
+def hand_on(x, dx, x_out, dx_out):
+    x_out[...] = x[...]
+    dx_out[...] = dx[...]
 
 
 def body(*args):
@@ -359,16 +408,17 @@
     weights = [(LEAF, LEAF)] * 2 + [(LEAF, RANK), (RANK, RANK)] + [(N_SIB - 1, RANK, RANK)] * 2 + [(NB_PAR, RANK, RANK)] * 2
     scratch = [V((RHS, 1, LEAF), f32)] * 2
     scratch += [V(w, f32) for w in weights]
-    for w in weights:
+    for w in weights[:4] + [(LEAF, 2 * RANK), (RANK, LEAF), (RANK, 2 * RANK)] + weights[4:]:
         scratch += [V(w, bf16)] * 2
     scratch += [
-        V((ITERS + 1, 2 * RHS, LEAF), f32),
+        V((ITERS, 2 * RHS, LEAF), f32),
+        V((2 * RHS, LEAF), f32),
         V((ITERS, 2 * RHS, RANK), f32),
         V((ITERS, N_SIB, 2 * RHS, RANK), f32),
         V((ITERS, N_SIB, 2 * ROWS, RANK), f32),
         V((ITERS, N_SIB - 1, 2 * ROWS, RANK), f32),
-        V((PARENTS, 2 * ROWS, RANK), f32),
-        V((PARENTS, 2 * ROWS, RANK), f32),
+        V((2, 2, N_Z, 2 * ROWS, RANK), f32),
+        V((2, 2, N_Z, 2 * ROWS, RANK), f32),
         V((ITERS, N_SIB, 2 * ROWS, RANK), f32),
         V((N_SIB, ROWS, 1, LEAF), f32),
         V((PARENTS, ROWS, LANES), f32),
@@ -380,9 +430,9 @@
     ]
     peers = N_SIB - 1
     scratch += [D((ITERS, 14)), D((ITERS, N_SIB, 2))] + [D((ITERS, peers))] * 4
-    scratch += [D((ITERS, N_Z - 1))] * 2 + [D((ITERS, N_Z))] * 2 + [D((ITERS, 2 * N_Z))] * 2
+    scratch += [D((ITERS, N_Z - 1))] * 2 + [D((ITERS, len(TO_XLO)))] * 2 + [D((ITERS, 2, len(TO_CORE)))] * 2
     scratch += [D((peers,))] * 6
-    return pl.pallas_call(
+    found = pl.pallas_call(
         kernel,
         out_shape=(out, out),
         in_specs=specs,
@@ -393,6 +443,10 @@
         ),
         name="richardson",
     )(*args)
+    whole = pl.BlockSpec(memory_space=pltpu.VMEM)
+    return pl.pallas_call(
+        hand_on, out_shape=(out, out), in_specs=[whole] * 2, out_specs=(whole, whole), name="hand_on"
+    )(*found)
 
 
 def solution(mesh):

time: 86.6 us -> 74.5 us (0.86)
  Pallas kernels: 82.5 us -> 73.8 us
  local copies, waits for them, and re-layouts: 3.34 us -> 0 us
    pallas_call x1, Pallas kernels: 82.5 us -> 71.9 us  [body(): pl.pallas_call(kernel, out_shape=(out, out), in_specs=specs, out_specs=(p...]
    unnamed x2 -> x0, local copies, waits for them, and re-layouts: 3.34 us -> none
    pallas_call x0 -> x1, Pallas kernels: none -> 1.91 us  [body(): pl.pallas_call(hand_on, out_shape=(out, out), in_specs=[whole] * 2, out_s...]
where the time goes in v3:
time: 74.5 us; the launch traced here: 74.4 us
  Pallas kernels  73.8 us (99%)
    pallas_call x1, Pallas kernels, body(): pl.pallas_call(kernel, out_shape=(out, out), in_specs=specs, out_specs=(p...  71.9 us
    pallas_call x1, Pallas kernels, body(): pl.pallas_call(hand_on, out_shape=(out, out), in_specs=[whole] * 2, out_s...  1.91 us

profile of v3, /device:TPU:1, one launch (start us, length us, event | category | flops | bytes accessed | tf_op | source)
XLA Modules:
  0.0 74.4 jit_solution(14902541126549203621)
XLA Ops:
  0.6 71.9 %richardson.1 = (f32[128,1,512]{2,1,0:T(1,128)}, f32[128,1,512]{2,1,0:T(1,128)}) custom-call(f32[128,1,512]{2,1,0:T(1,128)} %rhs_hbm.1, s32[1,512]{1,0:T(1,128)} %order_hbm.1, f32[128,1,512]{2,1,0:T(1,128)} %x_hbm.1, f32[128,1,512]{2,1,0:T(1,128)} %dx_hbm.1, f32[1,1,512,512]{3,2,1,0:T(8,128)} %dense_hbm.1, f32[1,1,512,512]{3,2,1,0:T(8,128)} %dense_d_hbm.1, ...), custom_call_target="tpu_custom_call" | custom-call | tf_op jit(solution)/shard_map/richardson/pallas_call | solution.py:435
  72.5 1.9 %hand_on.1 = (f32[128,1,512]{2,1,0:T(1,128)}, f32[128,1,512]{2,1,0:T(1,128)}) custom-call(f32[128,1,512]{2,1,0:T(1,128)} %get-tuple-element.4.x, f32[128,1,512]{2,1,0:T(1,128)} %get-tuple-element.5.dx), custom_call_target="tpu_custom_call" | custom-call | tf_op jit(solution)/shard_map/hand_on/pallas_call | solution.py:447

commit v4 on v3

--- a/solution.py
+++ b/solution.py
@@ -98,6 +98,58 @@
     load("trans", trans_hbm.at[0, 0], trans_in, 3)
     load("points", rhs_hbm.at[pl.ds(pl.multiple_of(me * ROWS, ROWS), ROWS)], points_in.at[me], 4)
     load("order", order_hbm, order.at[me], 5)
+
+    barrier = pltpu.get_barrier_semaphore()
+
+    def greet(device):
+        pl.semaphore_signal(barrier, inc=1, device_id=device, device_id_type=MESH)
+
+    for o in range(1, N_SIB):
+        greet(sib_dev(o))
+    for d in range(1, N_Z):
+        greet((me, parent(xlo, z + d, core)))
+    greet((me, parent(1 - xlo, z, core)))
+    greet((me, parent(xlo, z, 1 - core)))
+
+    sent = []
+
+    def send(src, dst, ssem, rsem, device):
+        c = pltpu.make_async_remote_copy(
+            src_ref=src, dst_ref=dst, send_sem=ssem, recv_sem=rsem, device_id=device, device_id_type=MESH
+        )
+        c.start()
+        sent.append(c)
+        return c
+
+    def arrived(buf, sem):
+        pltpu.make_async_copy(buf, buf, sem).wait()
+
+    def slot(dx, dy):
+        return dx % 2 * 4 + dy % 4
+
+    def split(src, high, low):
+        h, l = parts(src)
+        high[...] = h
+        low[...] = l
+
+    def coefficients(it):
+        v = parts(state[it])
+        c = product(v, (basis_h[...], basis_l[...]))
+        keep(it, c, product(parts(c), (trans_h[...], trans_l[...])))
+
+    def keep(it, c, t):
+        coeff[it] = c
+        for s in range(N_SIB):
+            term[it, s, :ROWS] = t[s * ROWS:(s + 1) * ROWS]
+            term[it, s, ROWS:] = t[RHS + s * ROWS:RHS + (s + 1) * ROWS]
+
+    loads["x"].wait()
+    state[0, :RHS] = x_in[...].reshape(RHS, LEAF)
+    loads["basis"].wait()
+    split(basis_in[...], basis_h, basis_l)
+    loads["dx"].wait()
+    state[0, RHS:] = dx_in[...].reshape(RHS, LEAF)
+    loads["trans"].wait()
     load("dense", dense_hbm.at[0, 0], dense_in, 6)
     load("dense_d", dense_d_hbm.at[0, 0], dense_d_in, 7)
     load("partners", partners_hbm, partners, 12)
@@ -105,58 +157,6 @@
     load("par_d", par_d_hbm.at[0], par_d_in, 9)
     load("sib_k", sib_k_hbm.at[0, 0], sib_k_in, 10)
     load("sib_d", sib_d_hbm.at[0, 0], sib_d_in, 11)
-
-    barrier = pltpu.get_barrier_semaphore()
-
-    def greet(device):
-        pl.semaphore_signal(barrier, inc=1, device_id=device, device_id_type=MESH)
-
-    for o in range(1, N_SIB):
-        greet(sib_dev(o))
-    for d in range(1, N_Z):
-        greet((me, parent(xlo, z + d, core)))
-    greet((me, parent(1 - xlo, z, core)))
-    greet((me, parent(xlo, z, 1 - core)))
-
-    sent = []
-
-    def send(src, dst, ssem, rsem, device):
-        c = pltpu.make_async_remote_copy(
-            src_ref=src, dst_ref=dst, send_sem=ssem, recv_sem=rsem, device_id=device, device_id_type=MESH
-        )
-        c.start()
-        sent.append(c)
-        return c
-
-    def arrived(buf, sem):
-        pltpu.make_async_copy(buf, buf, sem).wait()
-
-    def slot(dx, dy):
-        return dx % 2 * 4 + dy % 4
-
-    def split(src, high, low):
-        h, l = parts(src)
-        high[...] = h
-        low[...] = l
-
-    def coefficients(it):
-        v = parts(state[it])
-        c = product(v, (basis_h[...], basis_l[...]))
-        keep(it, c, product(parts(c), (trans_h[...], trans_l[...])))
-
-    def keep(it, c, t):
-        coeff[it] = c
-        for s in range(N_SIB):
-            term[it, s, :ROWS] = t[s * ROWS:(s + 1) * ROWS]
-            term[it, s, ROWS:] = t[RHS + s * ROWS:RHS + (s + 1) * ROWS]
-
-    loads["x"].wait()
-    state[0, :RHS] = x_in[...].reshape(RHS, LEAF)
-    loads["basis"].wait()
-    split(basis_in[...], basis_h, basis_l)
-    loads["dx"].wait()
-    state[0, RHS:] = dx_in[...].reshape(RHS, LEAF)
-    loads["trans"].wait()
     split(trans_in[...], trans_h, trans_l)
     coefficients(0)
 
@@ -167,15 +167,6 @@
         upper = (upper_0, upper_1)[it]
         for o in SIB_ORDER:
             send(term.at[it, sib_at(o)], term_in.at[it, o - 1], term_s.at[it, o - 1], term_r.at[it, o - 1], sib_dev(o))
-        if it == 0:
-            loads["points"].wait()
-            loads["order"].wait()
-            for o in SIB_ORDER:
-                send(order.at[me], order.at[me], order_s.at[o - 1], order_r.at[o - 1], sib_dev(o))
-                send(
-                    rhs_hbm.at[pl.ds(pl.multiple_of(sib_at(o) * ROWS, ROWS), ROWS)], points_in.at[me],
-                    rhs_s.at[o - 1], rhs_r.at[o - 1], sib_dev(o),
-                )
         gathered = []
 
         def piece(dx, dy, half):
@@ -224,6 +215,15 @@
                 (me, parent(xlo, z + d, core)),
             )
 
+        if it == 0:
+            loads["points"].wait()
+            loads["order"].wait()
+            for o in SIB_ORDER:
+                send(order.at[me], order.at[me], order_s.at[o - 1], order_r.at[o - 1], sib_dev(o))
+                send(
+                    rhs_hbm.at[pl.ds(pl.multiple_of(sib_at(o) * ROWS, ROWS), ROWS)], points_in.at[me],
+                    rhs_s.at[o - 1], rhs_r.at[o - 1], sib_dev(o),
+                )
         def to_xlo(k):
             run = upper.at[core, xlo, pl.ds(*TO_XLO[k])]
             send(run, run, xlo_s.at[it, k], xlo_r.at[it, k], (me, parent(1 - xlo, z, core)))
@@ -289,47 +289,52 @@
         if it == 0:
             loads["sib_k"].wait()
             loads["sib_d"].wait()
-        split_sib(0, 2)
+        split_sib(0, N_SIB - 1)
+        if it == 0:
+            both = product((basis_h[...], basis_l[...]), (trans_h[...], trans_l[...]))
+            split(jnp.concatenate([basis_in[...], both], axis=1), pair_h, pair_l)
+            split(both.T, lift_h, lift_l)
+            split(product((lift_h[...], lift_l[...]), (pair_h[...], pair_l[...])), turn_h, turn_l)
+
+        opposite(0)
         from_z(1)
         from_z(7)
         to_xlo(0)
         to_core(0, 0)
-        if it == 0:
-            points_here()
         from_z(2)
         to_xlo(1)
         from_z(6)
         to_xlo(2)
+        from_z(3)
+        to_xlo(3)
+        to_core(0, 1)
+        from_z(5)
+        to_xlo(4)
+        to_core(0, 2)
+        from_z(4)
+        to_xlo(5)
+        to_core(0, 3)
+        if it == 0:
+            points_here()
         place_two(0)
         from_xlo(0)
         to_core(1, 0)
-        opposite(0)
-        from_z(3)
-        to_xlo(3)
-        to_core(0, 1)
         place_two(1)
-        from_z(5)
-        to_xlo(4)
-        to_core(0, 2)
-        place_two(2)
-        from_z(4)
-        to_xlo(5)
-        to_core(0, 3)
-        opposite(1)
         from_xlo(1)
         from_xlo(3)
         to_core(1, 1)
+        place_two(2)
+        opposite(1)
+        from_xlo(2)
+        from_xlo(4)
+        to_core(1, 2)
         place_two(3)
         if it == 0:
             rhs[me] = placed[me]
             for o in SIB_ORDER:
                 send(placed.at[sib_at(o)], rhs.at[me], back_s.at[o - 1], back_r.at[o - 1], sib_dev(o))
-        from_xlo(2)
-        from_xlo(4)
-        to_core(1, 2)
         from_xlo(5)
         to_core(1, 3)
-        split_sib(2, N_SIB - 1)
         if it == 0:
             loads["partners"].wait()
         for far in range(2):
@@ -350,12 +355,6 @@
         field[it, me, ROWS:] = hd
         for o in SIB_ORDER:
             send(field.at[it, me], field.at[it, me], field_s.at[it, o - 1], field_r.at[it, o - 1], sib_dev(o))
-
-        if it == 0:
-            both = product((basis_h[...], basis_l[...]), (trans_h[...], trans_l[...]))
-            split(jnp.concatenate([basis_in[...], both], axis=1), pair_h, pair_l)
-            split(both.T, lift_h, lift_l)
-            split(product((lift_h[...], lift_l[...]), (pair_h[...], pair_l[...])), turn_h, turn_l)
 
         gx = jnp.zeros((2 * RHS, RANK), f32)
         gd = jnp.zeros((RHS, RANK), f32)

time: 74.5 us -> 73.9 us (level)
  no operation moved by 1% of the time
where the time goes in v4:
time: 73.9 us; the launch traced here: 73.7 us
  Pallas kernels  73.1 us (99%)
    pallas_call x1, Pallas kernels, body(): pl.pallas_call(kernel, out_shape=(out, out), in_specs=specs, out_specs=(p...  71.2 us
    pallas_call x1, Pallas kernels, body(): pl.pallas_call(hand_on, out_shape=(out, out), in_specs=[whole] * 2, out_s...  1.91 us

profile of v4, /device:TPU:1, one launch (start us, length us, event | category | flops | bytes accessed | tf_op | source)
XLA Modules:
  0.0 73.7 jit_solution(15431445131981938179)
XLA Ops:
  0.6 71.2 %richardson.1 = (f32[128,1,512]{2,1,0:T(1,128)}, f32[128,1,512]{2,1,0:T(1,128)}) custom-call(f32[128,1,512]{2,1,0:T(1,128)} %rhs_hbm.1, s32[1,512]{1,0:T(1,128)} %order_hbm.1, f32[128,1,512]{2,1,0:T(1,128)} %x_hbm.1, f32[128,1,512]{2,1,0:T(1,128)} %dx_hbm.1, f32[1,1,512,512]{3,2,1,0:T(8,128)} %dense_hbm.1, f32[1,1,512,512]{3,2,1,0:T(8,128)} %dense_d_hbm.1, ...), custom_call_target="tpu_custom_call" | custom-call | tf_op jit(solution)/shard_map/richardson/pallas_call | solution.py:434
  71.8 1.9 %hand_on.1 = (f32[128,1,512]{2,1,0:T(1,128)}, f32[128,1,512]{2,1,0:T(1,128)}) custom-call(f32[128,1,512]{2,1,0:T(1,128)} %get-tuple-element.4.x, f32[128,1,512]{2,1,0:T(1,128)} %get-tuple-element.5.dx), custom_call_target="tpu_custom_call" | custom-call | tf_op jit(solution)/shard_map/hand_on/pallas_call | solution.py:446

commit v5 on v4

--- a/solution.py
+++ b/solution.py
@@ -375,6 +375,11 @@
         ahead[RHS:] = known[RHS:]
         if not last:
             known_c = product(parts(ahead[...]), (pair_h[...], pair_l[...]))
+
+        if last:
+            for c in sent[:-(N_SIB - 1)]:
+                c.wait_send()
+            del sent[:-(N_SIB - 1)]
 
         for o in SIB_ORDER:
             arrived(field.at[it, sib_at(o)], field_r.at[it, N_SIB - o - 1])

time: 73.9 us -> 73.7 us (level)
  no operation moved by 1% of the time
where the time goes in v5:
time: 73.7 us; the launch traced here: 73.6 us
  Pallas kernels  72.9 us (99%)
    pallas_call x1, Pallas kernels, body(): pl.pallas_call(kernel, out_shape=(out, out), in_specs=specs, out_specs=(p...  71 us
    pallas_call x1, Pallas kernels, body(): pl.pallas_call(hand_on, out_shape=(out, out), in_specs=[whole] * 2, out_s...  1.91 us

profile of v5, /device:TPU:1, one launch (start us, length us, event | category | flops | bytes accessed | tf_op | source)
XLA Modules:
  0.0 73.6 jit_solution(3543574424702695047)
XLA Ops:
  0.6 71.0 %richardson.1 = (f32[128,1,512]{2,1,0:T(1,128)}, f32[128,1,512]{2,1,0:T(1,128)}) custom-call(f32[128,1,512]{2,1,0:T(1,128)} %rhs_hbm.1, s32[1,512]{1,0:T(1,128)} %order_hbm.1, f32[128,1,512]{2,1,0:T(1,128)} %x_hbm.1, f32[128,1,512]{2,1,0:T(1,128)} %dx_hbm.1, f32[1,1,512,512]{3,2,1,0:T(8,128)} %dense_hbm.1, f32[1,1,512,512]{3,2,1,0:T(8,128)} %dense_d_hbm.1, ...), custom_call_target="tpu_custom_call" | custom-call | tf_op jit(solution)/shard_map/richardson/pallas_call | solution.py:439
  71.7 1.9 %hand_on.1 = (f32[128,1,512]{2,1,0:T(1,128)}, f32[128,1,512]{2,1,0:T(1,128)}) custom-call(f32[128,1,512]{2,1,0:T(1,128)} %get-tuple-element.4.x, f32[128,1,512]{2,1,0:T(1,128)} %get-tuple-element.5.dx), custom_call_target="tpu_custom_call" | custom-call | tf_op jit(solution)/shard_map/hand_on/pallas_call | solution.py:451
